TPU v7x, 32 devices: a whole 2x2x4 slice. The times are simulated.
32 devices in a mesh: row: 4 (over y, core), col: 8 (over z, x).
Axes of the slice: x: 2, y: 2, z: 4, core: 2. Of those that a mesh axis runs over, the one named last changes fastest.
Arguments:
- inputs: bfloat16 [192, 8192], P('col', 'row'), may hold values from -6 to 6
- w_gate: bfloat16 [8192, 14336], P('row', 'col'), may hold values from -0.0625 to 0.0625
- w_up: bfloat16 [8192, 14336], P('row', 'col'), may hold values from -0.0625 to 0.0625
- w_down: bfloat16 [14336, 8192], P('col', 'row'), may hold values from -0.046875 to 0.046875
- cotangent: bfloat16 [192, 8192], P('col', 'row'), may hold values from -6 to 6
Outputs:
- grad_inputs: bfloat16 [192, 8192], P('col', 'row')
- grad_gate: bfloat16 [8192, 14336], P('row', 'col')
- grad_up: bfloat16 [8192, 14336], P('row', 'col')
- grad_down: bfloat16 [14336, 8192], P('col', 'row')
All inputs are finite; a program needn't handle non-finite values.
Results may differ from a plain program's by a relative error of at most 0.0049.
Values may be sent and summed in bfloat16 or wider, within the bound.
A program may use at most 128 MiB of HBM per device.

v0:
```python
import jax
import jax.numpy as jnp
from jax import lax
from jax.sharding import PartitionSpec as P


def contract_rows(left, right):
    return lax.dot_general(
        left, right, (((0,), (0,)), ((), ())), preferred_element_type=jnp.float32
    )


def contract_cols(left, right):
    return lax.dot_general(
        left, right, (((1,), (1,)), ((), ())), preferred_element_type=jnp.float32
    )


def on_device(inputs, w_gate, w_up, w_down, cotangent):
    all_inputs, all_cotangent = (
        lax.all_gather(inputs, "col", axis=0, tiled=True),
        lax.all_gather(cotangent, "col", axis=0, tiled=True),
    )
    columns = w_gate.shape[1]
    rows_in = all_inputs
    rows_co = all_cotangent
    gate_part = jnp.dot(rows_in, w_gate, preferred_element_type=jnp.float32)
    up_part = jnp.dot(rows_in, w_up, preferred_element_type=jnp.float32)
    back_part = contract_cols(rows_co, w_down)
    summed = lax.psum_scatter(
        jnp.concatenate([gate_part, up_part, back_part], axis=1),
        "row",
        scatter_dimension=0,
        tiled=True,
    )
    gate_sum = summed[:, :columns]
    up_sum = summed[:, columns : 2 * columns]
    grad_hidden = summed[:, 2 * columns :]
    sigmoid_gate = jax.nn.sigmoid(gate_sum)
    activated = gate_sum * sigmoid_gate
    hidden = (activated * up_sum).astype(jnp.bfloat16)
    grad_gate_act = (
        grad_hidden * up_sum * sigmoid_gate * (1.0 + gate_sum * (1.0 - sigmoid_gate))
    ).astype(jnp.bfloat16)
    grad_up_act = (grad_hidden * activated).astype(jnp.bfloat16)
    piece_gate = lax.all_gather(grad_gate_act, "row", axis=0, tiled=True)
    piece_up = lax.all_gather(grad_up_act, "row", axis=0, tiled=True)
    piece_hidden = lax.all_gather(hidden, "row", axis=0, tiled=True)
    rows_in = all_inputs
    rows_co = all_cotangent
    acc_gate = contract_rows(rows_in, piece_gate)
    acc_up = contract_rows(rows_in, piece_up)
    acc_down = contract_rows(piece_hidden, rows_co)
    input_rows = contract_cols(piece_gate, w_gate) + contract_cols(piece_up, w_up)
    acc_inputs = input_rows
    results = (acc_gate, acc_up, acc_down, acc_inputs)
    acc_gate, acc_up, acc_down, acc_inputs = results
    grad_inputs = lax.psum_scatter(acc_inputs, "col", scatter_dimension=0, tiled=True).astype(
        jnp.bfloat16
    )
    return (
        grad_inputs,
        acc_gate.astype(jnp.bfloat16),
        acc_up.astype(jnp.bfloat16),
        acc_down.astype(jnp.bfloat16),
    )


def solution(mesh):
    placed = (P("col", "row"), P("row", "col"), P("row", "col"), P("col", "row"), P("col", "row"))
    return jax.shard_map(
        on_device,
        mesh=mesh,
        in_specs=placed,
        out_specs=(P("col", "row"), P("row", "col"), P("row", "col"), P("col", "row")),
        check_vma=False,
    )
```

profile of v0, /device:TPU:0, one launch (start us, length us, event | category | flops | bytes accessed | tf_op | source)
XLA Modules:
  0.0 233.8 jit_solution(10962579120993300108)
XLA Ops:
  7.2 0.0 reduce-scatter.3.cloned.1.call-start
  7.2 0.0 slice-start
  7.2 34.2 %all_gather.15 = bf16[192,2048]{1,0:T(8,128)(2,1)S(1)} all-gather(bf16[24,2048]{1,0:T(8,128)(2,1)} %param.5), channel_id=1, replica_groups=mesh['row'=4,'col'=8] {'col'}, dimensions={0}, use_global_device_ids=true | all-gather | bytes 884736 | tf_op jit(solution)/shard_map/all_gather | solution.py:21
  41.4 4.8 %fusion.3 = f32[192,1792]{1,0:T(8,128)S(1)} fusion(bf16[192,2048]{1,0:T(8,128)(2,1)S(1)} %all_gather.15, bf16[2048,1792]{1,0:T(8,128)(2,1)} %param.6), kind=kOutput, calls=%fused_computation.12 | convolution fusion | flops 1409286144 | bytes 9502720 | tf_op jit(solution)/shard_map/dot_general | solution.py:27
  46.2 0.0 slice-done
  46.2 0.0 slice-done.1
  46.3 0.0 copy-start
  46.3 0.0 slice-start.3
  46.3 1.7 fusion.4
  48.0 0.0 copy-done
  48.0 32.1 %all_gather.16 = bf16[192,2048]{1,0:T(8,128)(2,1)S(1)} all-gather(bf16[24,2048]{1,0:T(8,128)(2,1)S(1)} %copy-done), channel_id=1, replica_groups=mesh['row'=4,'col'=8] {'col'}, dimensions={0}, use_global_device_ids=true | all-gather | bytes 884736 | tf_op jit(solution)/shard_map/all_gather | solution.py:22
  80.1 0.0 slice-done.2
  80.1 0.0 slice-done.3
  80.1 2.6 %fusion.5 = f32[192,1792]{1,0:T(8,128)S(1)} fusion(bf16[192,2048]{1,0:T(8,128)(2,1)S(1)} %all_gather.16, bf16[1792,2048]{1,0:T(8,128)(2,1)S(1)} %bitcast.23), kind=kOutput, calls=%fused_computation.14 | convolution fusion | flops 1409286144 | bytes 9502720 | tf_op jit(solution)/shard_map/dot_general | solution.py:14
  82.7 2.3 pad_maximum_fusion
  84.9 0.0 reduce-scatter.3.cloned.1.call-update
  84.9 0.0 reduce-scatter.5.cloned.1.call-start
  85.0 45.2 %reduce-scatter.3.cloned.1.call-done = f32[48,5376]{1,0:T(8,128)} async-done(((f32[192,5376]{1,0:T(8,128)}), f32[48,5376]{1,0:T(8,128)}) %reduce-scatter.3.cloned.1.call-update) | async-done | bytes 1032208 | tf_op jit(solution)/shard_map/reduce_scatter | solution.py:30
  130.2 1.4 multiply_convert_fusion
  131.6 7.7 %all_gather.17 = bf16[192,1792]{1,0:T(8,128)(2,1)S(1)} all-gather(bf16[48,1792]{1,0:T(8,128)(2,1)S(1)} %get-tuple-element.9), channel_id=1, replica_groups=mesh['row'=4,'col'=8] {'row'}, dimensions={0}, use_global_device_ids=true | all-gather | bytes 860160 | tf_op jit(solution)/shard_map/all_gather | solution.py:46
  139.2 5.6 %fusion.6 = f32[192,2048]{1,0:T(8,128)S(1)} fusion(bf16[192,1792]{1,0:T(8,128)(2,1)S(1)} %all_gather.17, bf16[2048,1792]{1,0:T(8,128)(2,1)} %param.6), kind=kOutput, calls=%fused_computation.15 | convolution fusion | flops 1409286144 | bytes 9601024 | tf_op jit(solution)/shard_map/dot_general | solution.py:14
  144.8 8.4 %all_gather.18 = bf16[192,1792]{1,0:T(8,128)(2,1)S(1)} all-gather(bf16[48,1792]{1,0:T(8,128)(2,1)S(1)} %get-tuple-element.10), channel_id=1, replica_groups=mesh['row'=4,'col'=8] {'row'}, dimensions={0}, use_global_device_ids=true | all-gather | bytes 860160 | tf_op jit(solution)/shard_map/all_gather | solution.py:47
  153.2 6.8 %convolution_add_fusion = f32[192,2048]{1,0:T(8,128)} fusion(f32[192,2048]{1,0:T(8,128)S(1)} %fusion.6, bf16[192,1792]{1,0:T(8,128)(2,1)S(1)} %all_gather.18, bf16[2048,1792]{1,0:T(8,128)(2,1)} %param.7), kind=kOutput, calls=%fused_computation.6 | convolution fusion | flops 1409679360 | bytes 11173888 | tf_op jit(solution)/shard_map/dot_general | solution.py:14
  160.0 0.0 reduce-scatter.5.cloned.1.call-update
  160.0 5.2 %fusion.1 = bf16[2048,1792]{0,1:T(8,128)(2,1)} fusion(bf16[192,1792]{1,0:T(8,128)(2,1)S(1)} %all_gather.18, bf16[192,2048]{1,0:T(8,128)(2,1)S(1)} %all_gather.15), kind=kOutput, calls=%fused_computation.4 | convolution fusion | flops 1412956160 | bytes 8814592 | tf_op jit(solution)/shard_map/dot_general | solution.py:8
  165.2 10.0 %copy.10 = bf16[2048,1792]{1,0:T(8,128)(2,1)} copy(bf16[2048,1792]{0,1:T(8,128)(2,1)} %fusion.1) | data formatting | bytes 14680064
  175.1 5.2 %fusion = bf16[2048,1792]{0,1:T(8,128)(2,1)} fusion(bf16[192,1792]{1,0:T(8,128)(2,1)S(1)} %all_gather.17, bf16[192,2048]{1,0:T(8,128)(2,1)S(1)} %all_gather.15), kind=kOutput, calls=%fused_computation.3 | convolution fusion | flops 1412956160 | bytes 8814592 | tf_op jit(solution)/shard_map/dot_general | solution.py:8
  180.3 10.0 %copy.9 = bf16[2048,1792]{1,0:T(8,128)(2,1)} copy(bf16[2048,1792]{0,1:T(8,128)(2,1)} %fusion) | data formatting | bytes 14680064
  190.2 8.2 %all_gather.19 = bf16[192,1792]{1,0:T(8,128)(2,1)S(1)} all-gather(bf16[48,1792]{1,0:T(8,128)(2,1)S(1)} %get-tuple-element.8), channel_id=1, replica_groups=mesh['row'=4,'col'=8] {'row'}, dimensions={0}, use_global_device_ids=true | all-gather | bytes 860160 | tf_op jit(solution)/shard_map/all_gather | solution.py:48
  198.4 5.2 %convolution_convert_fusion = bf16[1792,2048]{1,0:T(8,128)(2,1)} fusion(bf16[192,1792]{1,0:T(8,128)(2,1)S(1)} %all_gather.19, bf16[192,2048]{1,0:T(8,128)(2,1)S(1)} %all_gather.16), kind=kOutput, calls=%fused_computation | convolution fusion | flops 1412956160 | bytes 8814592 | tf_op jit(solution)/shard_map/dot_general | solution.py:8
  203.6 21.8 %reduce-scatter.5.cloned.1.call-done = f32[24,2048]{1,0:T(8,128)} async-done(((f32[192,2048]{1,0:T(8,128)}), f32[24,2048]{1,0:T(8,128)}) %reduce-scatter.5.cloned.1.call-update) | async-done | bytes 196624 | tf_op jit(solution)/shard_map/reduce_scatter | solution.py:58
  225.4 1.6 convert_element_type.29
  (4 shorter events, 0.0 us)
Async XLA Ops:
  7.2 123.0 %reduce-scatter.3.cloned.1.call-start = ((), (), s32[]{:S(2)}) async-start(), calls=%async_computation.2 | async-start | bytes 5160960 | tf_op jit(solution)/shard_map/reduce_scatter | solution.py:30
  7.2 39.0 %slice-start = ((s8[7340032]{0:T(1024)(128)(4,1)}), s8[4194304]{0:T(1024)(128)(4,1)S(1)}, s32[]{:S(2)}) async-start(s8[7340032]{0:T(1024)(128)(4,1)} %bitcast.20), calls=%async_computation.4 | async-start | bytes 8388608
  41.4 4.8 %slice-start.1 = ((s8[7340032]{0:T(1024)(128)(4,1)}), s8[3145728]{0:T(1024)(128)(4,1)S(1)}, s32[]{:S(2)}) async-start(s8[7340032]{0:T(1024)(128)(4,1)} %bitcast.20), calls=%async_computation.5 | async-start | bytes 6291456
  41.4 38.7 %slice-start.2 = ((s8[7340032]{0:T(1024)(128)(4,1)}), s8[4194304]{0:T(1024)(128)(4,1)S(1)}, s32[]{:S(2)}) async-start(s8[7340032]{0:T(1024)(128)(4,1)} %bitcast.22), calls=%async_computation.6 | async-start | bytes 8388608
  46.3 1.7 copy-start
  46.3 33.8 %slice-start.3 = ((s8[7340032]{0:T(1024)(128)(4,1)}), s8[3145728]{0:T(1024)(128)(4,1)S(1)}, s32[]{:S(2)}) async-start(s8[7340032]{0:T(1024)(128)(4,1)} %bitcast.22), calls=%async_computation.7 | async-start | bytes 6291456
  84.9 140.5 %reduce-scatter.5.cloned.1.call-start = ((), (), s32[]{:S(2)}) async-start(), calls=%async_computation.3 | async-start | bytes 1769472 | tf_op jit(solution)/shard_map/reduce_scatter | solution.py:58
Sparse Core Ops, SparseCore 0:
  85.1 45.0 reduce-scatter.2
  160.1 65.2 reduce-scatter.4
where the time goes:
time: 235 us; the launch traced here: 234 us
  blocking collectives  90.5 us (39%)
  waiting for transfers between devices  67 us (29%)
  matrix products  36.9 us (16%)
  local copies, waits for them, and re-layouts  19.9 us (8%)
  between operations  14.1 us (6%)
  other arithmetic  5.2 us (2%)
    reduce_scatter x1, waiting for transfers between devices, on_device(): lax.psum_scatter(jnp.concatenate([gate_part, up_part, back_part], axis=1)...  45.2 us
    all_gather x1, blocking collectives, on_device(): lax.all_gather(inputs, 'col', axis=0, tiled=True)  34.2 us
    all_gather x1, blocking collectives, on_device(): lax.all_gather(cotangent, 'col', axis=0, tiled=True)  32.1 us
    reduce_scatter x1, waiting for transfers between devices, on_device(): lax.psum_scatter(acc_inputs, 'col', scatter_dimension=0, tiled=True)  21.8 us
    unnamed x12, local copies, waits for them, and re-layouts  19.9 us
    dot_general x3, matrix products, contract_rows(): lax.dot_general(left, right, (((0,), (0,)), ((), ())), preferred_element_...  15.5 us
    dot_general x3, matrix products, contract_cols(): lax.dot_general(left, right, (((1,), (1,)), ((), ())), preferred_element_...  14.9 us
    all_gather x1, blocking collectives, on_device(): piece_up = lax.all_gather(grad_up_act, 'row', axis=0, tiled=True)  8.37 us
  transfers between devices with their start and end apart: 2, of which 2 were waited for; matrix products, arithmetic and copies ran while one was open for 15% of the time, Pallas kernels for 0%

commit v1 on v0

v1 whole, which is shorter than its diff:
```python
import jax
import jax.numpy as jnp
from jax import lax
from jax.experimental import pallas as pl
from jax.experimental.pallas import tpu as pltpu
from jax.sharding import PartitionSpec as P

MESH = pl.DeviceIdType.MESH
BF16, F32 = jnp.bfloat16, jnp.float32
TILE = 256


def contract_rows(left, right):
    return lax.dot_general(
        left, right, (((0,), (0,)), ((), ())), preferred_element_type=jnp.float32
    )


def contract_cols(left, right):
    return lax.dot_general(
        left, right, (((1,), (1,)), ((), ())), preferred_element_type=jnp.float32
    )


def activations(gate_sum, up_sum, grad_hidden):
    sigmoid_gate = jax.nn.sigmoid(gate_sum)
    activated = gate_sum * sigmoid_gate
    hidden = (activated * up_sum).astype(BF16)
    grad_gate_act = (
        grad_hidden * up_sum * sigmoid_gate * (1.0 + gate_sum * (1.0 - sigmoid_gate))
    ).astype(BF16)
    grad_up_act = (grad_hidden * activated).astype(BF16)
    return grad_gate_act, grad_up_act, hidden


def on_device(inputs, w_gate, w_up, w_down, cotangent):
    rows_in = lax.all_gather(inputs, "col", axis=0, tiled=True)
    rows_co = lax.all_gather(cotangent, "col", axis=0, tiled=True)
    columns = w_gate.shape[1]
    gate_part = jnp.dot(rows_in, w_gate, preferred_element_type=jnp.float32)
    up_part = jnp.dot(rows_in, w_up, preferred_element_type=jnp.float32)
    back_part = contract_cols(rows_co, w_down)
    summed = lax.psum_scatter(
        jnp.concatenate([gate_part, up_part, back_part], axis=1),
        "row",
        scatter_dimension=0,
        tiled=True,
    )
    acts = activations(
        summed[:, :columns], summed[:, columns : 2 * columns], summed[:, 2 * columns :]
    )
    piece_gate, piece_up, piece_hidden = [
        lax.all_gather(act, "row", axis=0, tiled=True) for act in acts
    ]
    acc_gate = contract_rows(rows_in, piece_gate)
    acc_up = contract_rows(rows_in, piece_up)
    acc_down = contract_rows(piece_hidden, rows_co)
    acc_inputs = contract_cols(piece_gate, w_gate) + contract_cols(piece_up, w_up)
    grad_inputs = lax.psum_scatter(acc_inputs, "col", scatter_dimension=0, tiled=True)
    return (
        grad_inputs.astype(BF16),
        acc_gate.astype(BF16),
        acc_up.astype(BF16),
        acc_down.astype(BF16),
    )


def block_kernel(
    in_ref, cot_ref, wg_hbm, wu_hbm, wd_hbm,
    x_out, c_out, act_out, gi_ref,
    got, wg, wu, wd, xs, cs, part, sib_got, y_send, y_got, act,
    keep, rx_send, rx_got, rz_send, rz_got,
    load_sem, out_sem, z_ss, z_rs, x_ss, x_rs, p_ss, p_rs, y_ss, y_rs, a_ss, a_rs,
    gx_ss, gx_rs, gz_ss, gz_rs,
):
    shard, width = in_ref.shape
    half = 4 * shard
    mine = half // 2
    tiles = wg.shape[1] // TILE
    r, c = lax.axis_index("row"), lax.axis_index("col")
    k, x, z = lax.rem(r, 2), lax.rem(c, 2), lax.div(c, 2)
    sibling = (r + 1 - 2 * k, c)
    over_y = (lax.rem(r + 2, 4), c)
    over_x = (r, c + 1 - 2 * x)
    flipped = [z, z + 1 - 2 * lax.rem(z, 2), lax.rem(z + 2, 4), 3 - z]
    over_z = [(r, 2 * f + x) for f in flipped]
    own_rows = pl.multiple_of(k * mine, 16)
    sib_rows = pl.multiple_of((1 - k) * mine, 16)

    loads = [
        pltpu.make_async_copy(src, dst, load_sem.at[i])
        for i, (src, dst) in enumerate(
            [(in_ref, got.at[0, 0]), (cot_ref, got.at[0, 1]), (wg_hbm, wg), (wu_hbm, wu), (wd_hbm, wd)]
        )
    ]
    for load in loads:
        load.start()

    barrier = pltpu.get_barrier_semaphore()
    partners = [sibling, over_y, over_x] + over_z[1:]
    for partner in partners:
        pl.semaphore_signal(barrier, inc=1, device_id=partner, device_id_type=MESH)
    pl.semaphore_wait(barrier, len(partners))

    def remote(src, dst, ss, rs, device):
        return pltpu.make_async_remote_copy(
            src_ref=src, dst_ref=dst, send_sem=ss, recv_sem=rs, device_id=device, device_id_type=MESH
        )

    to_z = [None] + [
        remote(got.at[0], got.at[2 * d], z_ss.at[d], z_rs.at[d], over_z[d]) for d in (1, 2, 3)
    ]
    to_x = [
        remote(got.at[2 * d], got.at[2 * d + 1], x_ss.at[d], x_rs.at[d], over_x) for d in range(4)
    ]

    loads[0].wait()
    loads[1].wait()
    to_z[1].start()
    to_x[0].start()
    to_z[1].wait_recv()
    to_x[1].start()
    to_z[1].wait_send()
    to_z[3].start()
    to_z[2].start()

    def settle(h):
        at = pl.ds(h * half, half)
        for i, whole in enumerate((xs, cs)):
            whole[at, :] = jnp.concatenate(
                [got[4 * h + s, i].astype(F32) for s in range(4)], axis=0
            ).astype(BF16)

    def to_sibling(h, j):
        return remote(
            part.at[h, j, :, pl.ds(sib_rows, mine), :], sib_got.at[h, j],
            p_ss.at[h, j], p_rs.at[h, j], sibling,
        )

    def to_y(h, j):
        return remote(y_send.at[h, j], y_got.at[h, j], y_ss.at[h, j], y_rs.at[h, j], over_y)

    def act_to_sibling(h, j):
        at = act.at[:, pl.ds(pl.multiple_of(h * half + own_rows, 16), mine), pl.ds(pl.multiple_of(j * TILE, TILE), TILE)]
        return remote(at, at, a_ss.at[h, j], a_rs.at[h, j], sibling)

    def forward(h):
        at = pl.ds(h * half, half)

        @pl.loop(0, tiles)
        def _(j):
            cols = pl.ds(pl.multiple_of(j * TILE, TILE), TILE)
            part[h, j, 0] = jnp.dot(xs[at, :], wg[:, cols], preferred_element_type=F32)
            part[h, j, 1] = jnp.dot(xs[at, :], wu[:, cols], preferred_element_type=F32)
            part[h, j, 2] = contract_cols(cs[at, :], wd[cols, :])
            to_sibling(h, j).start()

    def reduce_cores(h):
        @pl.loop(0, tiles)
        def _(j):
            to_sibling(h, j).wait_recv()
            total = part[h, j, :, pl.ds(own_rows, mine), :] + sib_got[h, j]
            part[h, j, :, pl.ds(own_rows, mine), :] = total
            y_send[h, j] = total.astype(BF16)
            to_y(h, j).start()

    def activate(h):
        @pl.loop(0, tiles)
        def _(j):
            to_y(h, j).wait_recv()
            total = part[h, j, :, pl.ds(own_rows, mine), :] + y_got[h, j].astype(F32)
            rows = pl.ds(pl.multiple_of(h * half + own_rows, 16), mine)
            cols = pl.ds(pl.multiple_of(j * TILE, TILE), TILE)
            for m, value in enumerate(activations(total[0], total[1], total[2])):
                act[m, rows, cols] = value
            act_to_sibling(h, j).start()

        @pl.loop(0, tiles)
        def _(j):
            act_to_sibling(h, j).wait_recv()

    def grad_to_x(d):
        return remote(rx_send.at[d], rx_got.at[d], gx_ss.at[d], gx_rs.at[d], over_x)

    def grad_to_z(d):
        return remote(rz_send.at[d], rz_got.at[d], gz_ss.at[d], gz_rs.at[d], over_z[d])

    def backward(h):
        at = pl.ds(h * half, half)

        @pl.loop(0, width // TILE)
        def _(j):
            cols = pl.ds(pl.multiple_of(j * TILE, TILE), TILE)
            grad = contract_cols(act[0, at, :], wg[cols, :]) + contract_cols(act[1, at, :], wu[cols, :])
            for e in range(2):
                d = 2 * h + e
                keep[d, :, cols] = grad[2 * e * shard : (2 * e + 1) * shard]
                rx_send[d, :, cols] = grad[(2 * e + 1) * shard : (2 * e + 2) * shard].astype(BF16)

        for e in range(2):
            grad_to_x(2 * h + e).start()

    def reduce_x(h):
        for e in range(2):
            d = 2 * h + e
            grad_to_x(d).wait_recv()
            total = keep[d] + rx_got[d].astype(F32)
            if d == 0:
                keep[d] = total
            else:
                rz_send[d] = total.astype(BF16)
                grad_to_z(d).start()

    to_x[0].wait_recv()
    to_x[1].wait_recv()
    settle(0)
    for load in loads[2:]:
        load.wait()
    forward(0)
    reduce_cores(0)
    to_z[3].wait_recv()
    to_x[3].start()
    to_z[2].wait_recv()
    to_x[2].start()
    to_x[3].wait_recv()
    to_x[2].wait_recv()
    settle(1)
    outs = [
        pltpu.make_async_copy(src, dst, out_sem.at[i])
        for i, (src, dst) in enumerate([(xs, x_out), (cs, c_out), (act, act_out)])
    ]
    outs[0].start()
    outs[1].start()
    forward(1)
    reduce_cores(1)
    activate(0)
    backward(0)
    reduce_x(0)
    activate(1)
    outs[2].start()
    backward(1)
    reduce_x(1)
    total = keep[0]
    for d in (1, 3, 2):
        grad_to_z(d).wait_recv()
        total += rz_got[d].astype(F32)
    gi_ref[...] = total.astype(BF16)

    for d in (1, 2, 3):
        grad_to_z(d).wait_send()
        if d > 1:
            to_z[d].wait_send()
    for d in range(4):
        to_x[d].wait_send()
        grad_to_x(d).wait_send()
    for h in range(2):
        @pl.loop(0, tiles)
        def _(j):
            to_sibling(h, j).wait_send()
            to_y(h, j).wait_send()
            act_to_sibling(h, j).wait_send()
    for out in outs:
        out.wait()


def fused(inputs, w_gate, w_up, w_down, cotangent):
    shard, width = inputs.shape
    columns = w_gate.shape[1]
    tokens = 8 * shard
    half, mine, tiles = tokens // 2, tokens // 4, columns // TILE
    dma = pltpu.SemaphoreType.DMA
    hbm = pl.BlockSpec(memory_space=pl.ANY)
    xs, cs, act, grad_inputs = pl.pallas_call(
        block_kernel,
        out_shape=(
            jax.ShapeDtypeStruct((tokens, width), BF16),
            jax.ShapeDtypeStruct((tokens, width), BF16),
            jax.ShapeDtypeStruct((3, tokens, columns), BF16),
            jax.ShapeDtypeStruct((shard, width), BF16),
        ),
        in_specs=[hbm] * 5,
        out_specs=(hbm, hbm, hbm, pl.BlockSpec(memory_space=pltpu.VMEM)),
        scratch_shapes=[
            pltpu.VMEM((8, 2, shard, width), BF16),
            pltpu.VMEM(w_gate.shape, BF16),
            pltpu.VMEM(w_up.shape, BF16),
            pltpu.VMEM(w_down.shape, BF16),
            pltpu.VMEM((tokens, width), BF16),
            pltpu.VMEM((tokens, width), BF16),
            pltpu.VMEM((2, tiles, 3, half, TILE), F32),
            pltpu.VMEM((2, tiles, 3, mine, TILE), F32),
            pltpu.VMEM((2, tiles, 3, mine, TILE), BF16),
            pltpu.VMEM((2, tiles, 3, mine, TILE), BF16),
            pltpu.VMEM((3, tokens, columns), BF16),
            pltpu.VMEM((4, shard, width), F32),
            pltpu.VMEM((4, shard, width), BF16),
            pltpu.VMEM((4, shard, width), BF16),
            pltpu.VMEM((4, shard, width), BF16),
            pltpu.VMEM((4, shard, width), BF16),
            dma((5,)), dma((3,)), dma((4,)), dma((4,)), dma((4,)), dma((4,)),
            dma((2, tiles)), dma((2, tiles)), dma((2, tiles)), dma((2, tiles)),
            dma((2, tiles)), dma((2, tiles)),
            dma((4,)), dma((4,)), dma((4,)), dma((4,)),
        ],
        compiler_params=pltpu.CompilerParams(
            collective_id=0, has_side_effects=True, vmem_limit_bytes=56 * 2**20
        ),
        name="swiglu_block",
    )(inputs, cotangent, w_gate, w_up, w_down)
    return (
        grad_inputs,
        contract_rows(xs, act[0]).astype(BF16),
        contract_rows(xs, act[1]).astype(BF16),
        contract_rows(act[2], cs).astype(BF16),
    )


def solution(mesh):
    placed = (P("col", "row"), P("row", "col"), P("row", "col"), P("col", "row"), P("col", "row"))
    small = mesh.shape["row"] == 4 and mesh.shape["col"] == 8
    return jax.shard_map(
        fused if small else on_device,
        mesh=mesh,
        in_specs=placed,
        out_specs=(P("col", "row"), P("row", "col"), P("row", "col"), P("col", "row")),
        check_vma=False,
    )
```

time: 235 us -> 94 us (0.40)
  blocking collectives: 90.5 us -> 0 us
  Pallas kernels: 0 us -> 74.1 us
  waiting for transfers between devices: 67 us -> 0 us
  matrix products: 36.9 us -> 17 us
  local copies, waits for them, and re-layouts: 19.9 us -> 0.65 us
  between operations: 14.1 us -> 0.66 us
  other arithmetic: 5.2 us -> 0 us
    all_gather x5 -> x0, blocking collectives: 90.5 us -> none  [the longest x1 34.2 us: on_device(): lax.all_gather(inputs, 'col', axis=0, tiled=True)]
    pallas_call x0 -> x1, Pallas kernels: none -> 74.1 us  [fused(): pl.pallas_call(block_kernel, out_shape=(jax.ShapeDtypeStruct((tokens, wid...]
    reduce_scatter x2 -> x0, waiting for transfers between devices: 67 us -> none  [the longest x1 45.2 us: on_device(): lax.psum_scatter(jnp.concatenate([gate_part, up_part, back_part], axis=1)...]
    dot_general x5 -> x0, matrix products: 21.4 us -> none  [the longest x3 14.9 us: contract_cols(): lax.dot_general(left, right, (((1,), (1,)), ((), ())), preferred_element_...]
    unnamed x12 -> x7, local copies, waits for them, and re-layouts: 19.9 us -> 0.65 us
    convert_element_type x2 -> x0, other arithmetic: 2.95 us -> none  [the longest x1 1.58 us: on_device(): lax.psum_scatter(acc_inputs, 'col', scatter_dimension=0, tiled=True)]
  transfers between devices with their start and end apart: 2 -> 0, of which waited for: 2 -> 0; matrix products, arithmetic and copies ran while one was open for 15% -> 0% of each run, Pallas kernels for 0% -> 0%
where the time goes in v1:
time: 94 us; the launch traced here: 92.4 us
  Pallas kernels  74.1 us (79%)
  matrix products  17 us (18%)
    pallas_call x1, Pallas kernels, fused(): pl.pallas_call(block_kernel, out_shape=(jax.ShapeDtypeStruct((tokens, wid...  74.1 us
    dot_general x3, matrix products, contract_rows(): lax.dot_general(left, right, (((0,), (0,)), ((), ())), preferred_element_...  17 us

profile of v1, /device:TPU:0, one launch (start us, length us, event | category | flops | bytes accessed | tf_op | source)
XLA Modules:
  0.0 92.4 jit_solution(7431964294367253900)
XLA Ops:
  0.6 74.1 %swiglu_block.1 = (bf16[192,2048]{1,0:T(8,128)(2,1)}, bf16[192,2048]{1,0:T(8,128)(2,1)}, bf16[3,192,1792]{2,1,0:T(8,128)(2,1)}, bf16[24,2048]{1,0:T(8,128)(2,1)}) custom-call(bf16[24,2048]{1,0:T(8,128)(2,1)} %in_ref.1, bf16[24,2048]{1,0:T(8,128)(2,1)} %cot_ref.1, bf16[2048,1792]{1,0:T(8,128)(2,1)} %wg_hbm.1, bf16[2048,1792]{1,0:T(8,128)(2,1)} %wu_hbm.1, ...), custom_call_target="tpu_custom_call" | custom-call | tf_op jit(solution)/shard_map/swiglu_block/pallas_call | solution.py:273
  74.7 0.0 copy-start
  74.7 0.0 copy-start.1
  74.7 6.7 %convolution_convert_fusion = bf16[1792,2048]{1,0:T(8,128)(2,1)} fusion(bf16[192,2048]{1,0:T(8,128)(2,1)} %get-tuple-element.11, bf16[3,192,1792]{2,1,0:T(8,128)(2,1)} %get-tuple-element.10), kind=kOutput, calls=%fused_computation | convolution fusion | flops 1412956160 | bytes 8814592 | tf_op jit(solution)/shard_map/dot_general | solution.py:14
  81.4 0.0 copy-done
  81.4 0.0 copy-done.1
  81.4 5.2 %convolution_convert_fusion.1 = bf16[2048,1792]{1,0:T(8,128)(2,1)} fusion(bf16[192,2048]{1,0:T(8,128)(2,1)S(1)} %copy-done, bf16[3,192,1792]{2,1,0:T(8,128)(2,1)S(1)} %copy-done.1), kind=kOutput, calls=%fused_computation.1 | convolution fusion | flops 1412956160 | bytes 8814592 | tf_op jit(solution)/shard_map/dot_general | solution.py:14
  86.6 0.0 copy-start.2
  86.6 5.2 %convolution_convert_fusion.2 = bf16[2048,1792]{1,0:T(8,128)(2,1)} fusion(bf16[192,2048]{1,0:T(8,128)(2,1)S(1)} %copy-done, bf16[3,192,1792]{2,1,0:T(8,128)(2,1)S(1)} %copy-done.1), kind=kOutput, calls=%fused_computation.2 | convolution fusion | flops 1412956160 | bytes 8814592 | tf_op jit(solution)/shard_map/dot_general | solution.py:14
  91.8 0.0 copy-done.2
  91.8 0.6 copy.10
Async XLA Ops:
  74.7 6.7 %copy-start = (bf16[192,2048]{1,0:T(8,128)(2,1)S(1)}, bf16[192,2048]{1,0:T(8,128)(2,1)}, u32[]{:S(2)}) copy-start(bf16[192,2048]{1,0:T(8,128)(2,1)} %get-tuple-element.9) | copy-start | bytes 2359300
  74.7 6.7 %copy-start.1 = (bf16[3,192,1792]{2,1,0:T(8,128)(2,1)S(1)}, bf16[3,192,1792]{2,1,0:T(8,128)(2,1)}, u32[]{:S(2)}) copy-start(bf16[3,192,1792]{2,1,0:T(8,128)(2,1)} %get-tuple-element.10) | copy-start | bytes 6193156
  86.6 5.2 %copy-start.2 = (bf16[24,2048]{1,0:T(8,128)(2,1)S(1)}, bf16[24,2048]{1,0:T(8,128)(2,1)}, u32[]{:S(2)}) copy-start(bf16[24,2048]{1,0:T(8,128)(2,1)} %get-tuple-element.16) | copy-start | bytes 294916

commit v2 on v1

--- a/solution.py
+++ b/solution.py
@@ -69,7 +69,7 @@
     in_ref, cot_ref, wg_hbm, wu_hbm, wd_hbm,
     x_out, c_out, act_out, gi_ref,
     got, wg, wu, wd, xs, cs, part, sib_got, y_send, y_got, act,
-    keep, rx_send, rx_got, rz_send, rz_got,
+    grads, keep, rx_send, rx_got, rz_send, rz_got,
     load_sem, out_sem, z_ss, z_rs, x_ss, x_rs, p_ss, p_rs, y_ss, y_rs, a_ss, a_rs,
     gx_ss, gx_rs, gz_ss, gz_rs,
 ):
@@ -107,22 +107,46 @@
             src_ref=src, dst_ref=dst, send_sem=ss, recv_sem=rs, device_id=device, device_id_type=MESH
         )
 
-    to_z = [None] + [
-        remote(got.at[0], got.at[2 * d], z_ss.at[d], z_rs.at[d], over_z[d]) for d in (1, 2, 3)
-    ]
+    middle = jnp.logical_and(z > 0, z < 3)
+    own_near = remote(got.at[0], got.at[2], z_ss.at[0], z_rs.at[1], over_z[1])
+    own_far = remote(got.at[0], got.at[6], z_ss.at[1], z_rs.at[3], over_z[3])
+    near_far = remote(got.at[2], got.at[4], z_ss.at[2], z_rs.at[2], over_z[3])
+    far_near = remote(got.at[6], got.at[4], z_ss.at[3], z_rs.at[2], over_z[1])
+    last_near = remote(got.at[4], got.at[6], z_ss.at[4], z_rs.at[3], over_z[1])
     to_x = [
         remote(got.at[2 * d], got.at[2 * d + 1], x_ss.at[d], x_rs.at[d], over_x) for d in range(4)
     ]
 
     loads[0].wait()
     loads[1].wait()
-    to_z[1].start()
+    own_near.start()
+
+    @pl.when(middle)
+    def _():
+        own_far.start()
+
     to_x[0].start()
-    to_z[1].wait_recv()
+    own_near.wait_recv()
+
+    @pl.when(middle)
+    def _():
+        near_far.start()
+
     to_x[1].start()
-    to_z[1].wait_send()
-    to_z[3].start()
-    to_z[2].start()
+
+    @pl.when(middle)
+    def _():
+        own_far.wait_recv()
+        far_near.start()
+        to_x[3].start()
+        near_far.wait_recv()
+        last_near.start()
+        to_x[2].start()
+
+    @pl.when(jnp.logical_not(middle))
+    def _():
+        near_far.wait_recv()
+        to_x[2].start()
 
     def settle(h):
         at = pl.ds(h * half, half)
@@ -144,10 +168,10 @@
         at = act.at[:, pl.ds(pl.multiple_of(h * half + own_rows, 16), mine), pl.ds(pl.multiple_of(j * TILE, TILE), TILE)]
         return remote(at, at, a_ss.at[h, j], a_rs.at[h, j], sibling)
 
-    def forward(h):
+    def forward(h, first, last):
         at = pl.ds(h * half, half)
 
-        @pl.loop(0, tiles)
+        @pl.loop(first, last)
         def _(j):
             cols = pl.ds(pl.multiple_of(j * TILE, TILE), TILE)
             part[h, j, 0] = jnp.dot(xs[at, :], wg[:, cols], preferred_element_type=F32)
@@ -164,44 +188,48 @@
             y_send[h, j] = total.astype(BF16)
             to_y(h, j).start()
 
-    def activate(h):
-        @pl.loop(0, tiles)
-        def _(j):
-            to_y(h, j).wait_recv()
-            total = part[h, j, :, pl.ds(own_rows, mine), :] + y_got[h, j].astype(F32)
-            rows = pl.ds(pl.multiple_of(h * half + own_rows, 16), mine)
-            cols = pl.ds(pl.multiple_of(j * TILE, TILE), TILE)
-            for m, value in enumerate(activations(total[0], total[1], total[2])):
-                act[m, rows, cols] = value
-            act_to_sibling(h, j).start()
-
-        @pl.loop(0, tiles)
-        def _(j):
-            act_to_sibling(h, j).wait_recv()
-
     def grad_to_x(d):
         return remote(rx_send.at[d], rx_got.at[d], gx_ss.at[d], gx_rs.at[d], over_x)
 
     def grad_to_z(d):
         return remote(rz_send.at[d], rz_got.at[d], gz_ss.at[d], gz_rs.at[d], over_z[d])
 
+    def activate(h, j):
+        to_y(h, j).wait_recv()
+        total = part[h, j, :, pl.ds(own_rows, mine), :] + y_got[h, j].astype(F32)
+        rows = pl.ds(pl.multiple_of(h * half + own_rows, 16), mine)
+        cols = pl.ds(pl.multiple_of(j * TILE, TILE), TILE)
+        for m, value in enumerate(activations(total[0], total[1], total[2])):
+            act[m, rows, cols] = value
+        act_to_sibling(h, j).start()
+
+    def accumulate(h, j):
+        act_to_sibling(h, j).wait_recv()
+        cols = pl.ds(pl.multiple_of(j * TILE, TILE), TILE)
+        grad_gate = act[0, pl.ds(h * half, half), cols]
+        grad_up = act[1, pl.ds(h * half, half), cols]
+        for n in range(width // TILE):
+            out = pl.ds(n * TILE, TILE)
+            grads[:, out] += contract_cols(grad_gate, wg[out, cols]) + contract_cols(grad_up, wu[out, cols])
+
     def backward(h):
-        at = pl.ds(h * half, half)
-
-        @pl.loop(0, width // TILE)
+        grads[...] = jnp.zeros_like(grads)
+        activate(h, 0)
+
+        @pl.loop(1, tiles)
         def _(j):
-            cols = pl.ds(pl.multiple_of(j * TILE, TILE), TILE)
-            grad = contract_cols(act[0, at, :], wg[cols, :]) + contract_cols(act[1, at, :], wu[cols, :])
-            for e in range(2):
-                d = 2 * h + e
-                keep[d, :, cols] = grad[2 * e * shard : (2 * e + 1) * shard]
-                rx_send[d, :, cols] = grad[(2 * e + 1) * shard : (2 * e + 2) * shard].astype(BF16)
-
-        for e in range(2):
-            grad_to_x(2 * h + e).start()
+            activate(h, j)
+            accumulate(h, j - 1)
+
+        accumulate(h, tiles - 1)
+        for e in (1, 0):
+            d = 2 * h + e
+            rx_send[d] = grads[(2 * e + 1) * shard : (2 * e + 2) * shard, :].astype(BF16)
+            grad_to_x(d).start()
+            keep[d] = grads[2 * e * shard : (2 * e + 1) * shard, :]
 
     def reduce_x(h):
-        for e in range(2):
+        for e in (1, 0):
             d = 2 * h + e
             grad_to_x(d).wait_recv()
             total = keep[d] + rx_got[d].astype(F32)
@@ -216,12 +244,15 @@
     settle(0)
     for load in loads[2:]:
         load.wait()
-    forward(0)
+    forward(0, 0, tiles // 2)
+
+    @pl.when(jnp.logical_not(middle))
+    def _():
+        own_far.wait_recv()
+        to_x[3].start()
+
+    forward(0, tiles // 2, tiles)
     reduce_cores(0)
-    to_z[3].wait_recv()
-    to_x[3].start()
-    to_z[2].wait_recv()
-    to_x[2].start()
     to_x[3].wait_recv()
     to_x[2].wait_recv()
     settle(1)
@@ -231,14 +262,12 @@
     ]
     outs[0].start()
     outs[1].start()
-    forward(1)
+    forward(1, 0, tiles)
     reduce_cores(1)
-    activate(0)
     backward(0)
     reduce_x(0)
-    activate(1)
+    backward(1)
     outs[2].start()
-    backward(1)
     reduce_x(1)
     total = keep[0]
     for d in (1, 3, 2):
@@ -246,10 +275,15 @@
         total += rz_got[d].astype(F32)
     gi_ref[...] = total.astype(BF16)
 
+    own_near.wait_send()
+
+    @pl.when(middle)
+    def _():
+        for copy in (own_far, near_far, far_near, last_near):
+            copy.wait_send()
+
     for d in (1, 2, 3):
         grad_to_z(d).wait_send()
-        if d > 1:
-            to_z[d].wait_send()
     for d in range(4):
         to_x[d].wait_send()
         grad_to_x(d).wait_send()
@@ -261,6 +295,49 @@
             act_to_sibling(h, j).wait_send()
     for out in outs:
         out.wait()
+
+
+def weights_kernel(xs, cs, act, gate_hbm, up_hbm, down_hbm, gate_buf, up_buf, down_buf, sem):
+    blocks, down_blocks = xs.shape[1] // TILE, act.shape[2] // TILE
+
+    def writes(i):
+        at = pl.ds(pl.multiple_of(i * TILE, TILE), TILE)
+        slot = lax.rem(i, 2)
+        return [
+            pltpu.make_async_copy(buf.at[slot], hbm.at[at, :], sem.at[n, slot])
+            for n, (buf, hbm) in enumerate([(gate_buf, gate_hbm), (up_buf, up_hbm), (down_buf, down_hbm)])
+        ]
+
+    def block(i, count):
+        at = pl.ds(pl.multiple_of(i * TILE, TILE), TILE)
+        slot = lax.rem(i, 2)
+        copies = writes(i)[:count]
+
+        @pl.when(i >= 2)
+        def _():
+            for copy in writes(i - 2)[:count]:
+                copy.wait()
+
+        rows = xs[:, at].T
+        gate_buf[slot] = jnp.dot(rows, act[0], preferred_element_type=F32).astype(BF16)
+        copies[0].start()
+        up_buf[slot] = jnp.dot(rows, act[1], preferred_element_type=F32).astype(BF16)
+        copies[1].start()
+        if count == 3:
+            down_buf[slot] = jnp.dot(act[2, :, at].T, cs[...], preferred_element_type=F32).astype(BF16)
+            copies[2].start()
+
+    @pl.loop(0, down_blocks)
+    def _(i):
+        block(i, 3)
+
+    for i in range(down_blocks, blocks):
+        block(jnp.int32(i), 2)
+    for i in (blocks - 2, blocks - 1):
+        for copy in writes(jnp.int32(i))[:2]:
+            copy.wait()
+    for i in (down_blocks - 2, down_blocks - 1):
+        writes(jnp.int32(i))[2].wait()
 
 
 def fused(inputs, w_gate, w_up, w_down, cotangent):
@@ -292,12 +369,13 @@
             pltpu.VMEM((2, tiles, 3, mine, TILE), BF16),
             pltpu.VMEM((2, tiles, 3, mine, TILE), BF16),
             pltpu.VMEM((3, tokens, columns), BF16),
+            pltpu.VMEM((half, width), F32),
             pltpu.VMEM((4, shard, width), F32),
             pltpu.VMEM((4, shard, width), BF16),
             pltpu.VMEM((4, shard, width), BF16),
             pltpu.VMEM((4, shard, width), BF16),
             pltpu.VMEM((4, shard, width), BF16),
-            dma((5,)), dma((3,)), dma((4,)), dma((4,)), dma((4,)), dma((4,)),
+            dma((5,)), dma((3,)), dma((5,)), dma((4,)), dma((4,)), dma((4,)),
             dma((2, tiles)), dma((2, tiles)), dma((2, tiles)), dma((2, tiles)),
             dma((2, tiles)), dma((2, tiles)),
             dma((4,)), dma((4,)), dma((4,)), dma((4,)),
@@ -307,12 +385,26 @@
         ),
         name="swiglu_block",
     )(inputs, cotangent, w_gate, w_up, w_down)
-    return (
-        grad_inputs,
-        contract_rows(xs, act[0]).astype(BF16),
-        contract_rows(xs, act[1]).astype(BF16),
-        contract_rows(act[2], cs).astype(BF16),
-    )
+    vmem = pl.BlockSpec(memory_space=pltpu.VMEM)
+    grad_gate, grad_up, grad_down = pl.pallas_call(
+        weights_kernel,
+        out_shape=(
+            jax.ShapeDtypeStruct((width, columns), BF16),
+            jax.ShapeDtypeStruct((width, columns), BF16),
+            jax.ShapeDtypeStruct((columns, width), BF16),
+        ),
+        in_specs=[vmem] * 3,
+        out_specs=(hbm,) * 3,
+        scratch_shapes=[
+            pltpu.VMEM((2, TILE, columns), BF16),
+            pltpu.VMEM((2, TILE, columns), BF16),
+            pltpu.VMEM((2, TILE, width), BF16),
+            dma((3, 2)),
+        ],
+        compiler_params=pltpu.CompilerParams(vmem_limit_bytes=40 * 2**20),
+        name="weight_grads",
+    )(xs, cs, act)
+    return grad_inputs, grad_gate, grad_up, grad_down
 
 
 def solution(mesh):

time: 94 us -> 83.9 us (0.89); the launches traced: 92.4 us -> 83.6 us
  matrix products: 17 us -> 0 us
  local copies, waits for them, and re-layouts: 0.65 us -> 5.38 us
  Pallas kernels: 74.1 us -> 77.6 us
    dot_general x3 -> x0, matrix products: 17 us -> none  [contract_rows(): lax.dot_general(left, right, (((0,), (0,)), ((), ())), preferred_element_...]
    pallas_call x0 -> x1, Pallas kernels: none -> 8.66 us  [fused(): pl.pallas_call(weights_kernel, out_shape=(jax.ShapeDtypeStruct((width, co...]
    pallas_call x1, Pallas kernels: 74.1 us -> 68.9 us  [fused(): pl.pallas_call(block_kernel, out_shape=(jax.ShapeDtypeStruct((tokens, wid...]
    unnamed x7, local copies, waits for them, and re-layouts: 0.65 us -> 5.38 us
where the time goes in v2:
time: 83.9 us; the launch traced here: 83.6 us
  Pallas kernels  77.6 us (92%)
  local copies, waits for them, and re-layouts  5.38 us (6%)
    pallas_call x1, Pallas kernels, fused(): pl.pallas_call(block_kernel, out_shape=(jax.ShapeDtypeStruct((tokens, wid...  68.9 us
    pallas_call x1, Pallas kernels, fused(): pl.pallas_call(weights_kernel, out_shape=(jax.ShapeDtypeStruct((width, co...  8.66 us
    unnamed x7, local copies, waits for them, and re-layouts  5.38 us

profile of v2, /device:TPU:0, one launch (start us, length us, event | category | flops | bytes accessed | tf_op | source)
XLA Modules:
  0.0 83.6 jit_solution(3047720425562517514)
XLA Ops:
  0.6 68.9 %swiglu_block.1 = (bf16[192,2048]{1,0:T(8,128)(2,1)}, bf16[192,2048]{1,0:T(8,128)(2,1)}, bf16[3,192,1792]{2,1,0:T(8,128)(2,1)}, bf16[24,2048]{1,0:T(8,128)(2,1)}) custom-call(bf16[24,2048]{1,0:T(8,128)(2,1)} %in_ref.1, bf16[24,2048]{1,0:T(8,128)(2,1)} %cot_ref.1, bf16[2048,1792]{1,0:T(8,128)(2,1)} %wg_hbm.1, bf16[2048,1792]{1,0:T(8,128)(2,1)} %wu_hbm.1, ...), custom_call_target="tpu_custom_call" | custom-call | tf_op jit(solution)/shard_map/swiglu_block/pallas_call | solution.py:350
  69.5 0.0 copy-start
  69.6 1.6 %copy-done = bf16[3,192,1792]{2,1,0:T(8,128)(2,1)S(1)} copy-done((bf16[3,192,1792]{2,1,0:T(8,128)(2,1)S(1)}, bf16[3,192,1792]{2,1,0:T(8,128)(2,1)}, u32[]{:S(2)}) %copy-start) | copy-done | bytes 2064408
  71.1 0.0 copy-start.1
  71.1 1.1 %copy-done.1 = bf16[192,2048]{1,0:T(8,128)(2,1)S(1)} copy-done((bf16[192,2048]{1,0:T(8,128)(2,1)S(1)}, bf16[192,2048]{1,0:T(8,128)(2,1)}, u32[]{:S(2)}) %copy-start.1) | copy-done | bytes 786456
  72.3 0.0 copy-start.2
  72.3 1.1 %copy-done.2 = bf16[192,2048]{1,0:T(8,128)(2,1)S(1)} copy-done((bf16[192,2048]{1,0:T(8,128)(2,1)S(1)}, bf16[192,2048]{1,0:T(8,128)(2,1)}, u32[]{:S(2)}) %copy-start.2) | copy-done | bytes 786456
  73.4 8.7 %weight_grads.1 = (bf16[2048,1792]{1,0:T(8,128)(2,1)}, bf16[2048,1792]{1,0:T(8,128)(2,1)}, bf16[1792,2048]{1,0:T(8,128)(2,1)}) custom-call(bf16[192,2048]{1,0:T(8,128)(2,1)S(1)} %copy-done.1, bf16[192,2048]{1,0:T(8,128)(2,1)S(1)} %copy-done.2, bf16[3,192,1792]{2,1,0:T(8,128)(2,1)S(1)} %copy-done), custom_call_target="tpu_custom_call" | custom-call | tf_op jit(solution)/shard_map/weight_grads/pallas_call | solution.py:389
  82.1 1.5 %copy.10 = bf16[24,2048]{1,0:T(8,128)(2,1)} copy(bf16[24,2048]{1,0:T(8,128)(2,1)} %get-tuple-element.22) | data formatting | bytes 196608
Async XLA Ops:
  69.5 1.6 %copy-start = (bf16[3,192,1792]{2,1,0:T(8,128)(2,1)S(1)}, bf16[3,192,1792]{2,1,0:T(8,128)(2,1)}, u32[]{:S(2)}) copy-start(bf16[3,192,1792]{2,1,0:T(8,128)(2,1)} %get-tuple-element.14.act) | copy-start | bytes 6193156
  71.1 1.1 %copy-start.1 = (bf16[192,2048]{1,0:T(8,128)(2,1)S(1)}, bf16[192,2048]{1,0:T(8,128)(2,1)}, u32[]{:S(2)}) copy-start(bf16[192,2048]{1,0:T(8,128)(2,1)} %get-tuple-element.12.xs) | copy-start | bytes 2359300
  72.3 1.1 %copy-start.2 = (bf16[192,2048]{1,0:T(8,128)(2,1)S(1)}, bf16[192,2048]{1,0:T(8,128)(2,1)}, u32[]{:S(2)}) copy-start(bf16[192,2048]{1,0:T(8,128)(2,1)} %get-tuple-element.13.cs) | copy-start | bytes 2359300

commit v3 on v2

--- a/solution.py
+++ b/solution.py
@@ -1,3 +1,5 @@
+import functools
+
 import jax
 import jax.numpy as jnp
 from jax import lax
@@ -67,7 +69,7 @@
 
 def block_kernel(
     in_ref, cot_ref, wg_hbm, wu_hbm, wd_hbm,
-    x_out, c_out, act_out, gi_ref,
+    x_out, c_out, act_out, own_ref, two_ref, three_ref,
     got, wg, wu, wd, xs, cs, part, sib_got, y_send, y_got, act,
     grads, keep, rx_send, rx_got, rz_send, rz_got,
     load_sem, out_sem, z_ss, z_rs, x_ss, x_rs, p_ss, p_rs, y_ss, y_rs, a_ss, a_rs,
@@ -97,7 +99,7 @@
         load.start()
 
     barrier = pltpu.get_barrier_semaphore()
-    partners = [sibling, over_y, over_x] + over_z[1:]
+    partners = [sibling, over_y, over_x, over_z[1], over_z[3]]
     for partner in partners:
         pl.semaphore_signal(barrier, inc=1, device_id=partner, device_id_type=MESH)
     pl.semaphore_wait(barrier, len(partners))
@@ -191,8 +193,7 @@
     def grad_to_x(d):
         return remote(rx_send.at[d], rx_got.at[d], gx_ss.at[d], gx_rs.at[d], over_x)
 
-    def grad_to_z(d):
-        return remote(rz_send.at[d], rz_got.at[d], gz_ss.at[d], gz_rs.at[d], over_z[d])
+    grad_to_z = remote(rz_send, rz_got, gz_ss, gz_rs, over_z[1])
 
     def activate(h, j):
         to_y(h, j).wait_recv()
@@ -235,9 +236,11 @@
             total = keep[d] + rx_got[d].astype(F32)
             if d == 0:
                 keep[d] = total
+            elif d == 1:
+                rz_send[...] = total.astype(BF16)
+                grad_to_z.start()
             else:
-                rz_send[d] = total.astype(BF16)
-                grad_to_z(d).start()
+                (two_ref if d == 2 else three_ref)[...] = total.astype(BF16)
 
     to_x[0].wait_recv()
     to_x[1].wait_recv()
@@ -269,12 +272,8 @@
     backward(1)
     outs[2].start()
     reduce_x(1)
-    total = keep[0]
-    for d in (1, 3, 2):
-        grad_to_z(d).wait_recv()
-        total += rz_got[d].astype(F32)
-    gi_ref[...] = total.astype(BF16)
-
+    grad_to_z.wait_recv()
+    own_ref[...] = keep[0] + rz_got[...].astype(F32)
     own_near.wait_send()
 
     @pl.when(middle)
@@ -282,8 +281,7 @@
         for copy in (own_far, near_far, far_near, last_near):
             copy.wait_send()
 
-    for d in (1, 2, 3):
-        grad_to_z(d).wait_send()
+    grad_to_z.wait_send()
     for d in range(4):
         to_x[d].wait_send()
         grad_to_x(d).wait_send()
@@ -297,47 +295,16 @@
         out.wait()
 
 
-def weights_kernel(xs, cs, act, gate_hbm, up_hbm, down_hbm, gate_buf, up_buf, down_buf, sem):
-    blocks, down_blocks = xs.shape[1] // TILE, act.shape[2] // TILE
-
-    def writes(i):
+def weights_kernel(xs, cs, act, gate, up, down, *, down_blocks):
+    i = pl.program_id(0)
+    rows = xs[...].T
+    gate[...] = jnp.dot(rows, act[0], preferred_element_type=F32).astype(BF16)
+    up[...] = jnp.dot(rows, act[1], preferred_element_type=F32).astype(BF16)
+
+    @pl.when(i < down_blocks)
+    def _():
         at = pl.ds(pl.multiple_of(i * TILE, TILE), TILE)
-        slot = lax.rem(i, 2)
-        return [
-            pltpu.make_async_copy(buf.at[slot], hbm.at[at, :], sem.at[n, slot])
-            for n, (buf, hbm) in enumerate([(gate_buf, gate_hbm), (up_buf, up_hbm), (down_buf, down_hbm)])
-        ]
-
-    def block(i, count):
-        at = pl.ds(pl.multiple_of(i * TILE, TILE), TILE)
-        slot = lax.rem(i, 2)
-        copies = writes(i)[:count]
-
-        @pl.when(i >= 2)
-        def _():
-            for copy in writes(i - 2)[:count]:
-                copy.wait()
-
-        rows = xs[:, at].T
-        gate_buf[slot] = jnp.dot(rows, act[0], preferred_element_type=F32).astype(BF16)
-        copies[0].start()
-        up_buf[slot] = jnp.dot(rows, act[1], preferred_element_type=F32).astype(BF16)
-        copies[1].start()
-        if count == 3:
-            down_buf[slot] = jnp.dot(act[2, :, at].T, cs[...], preferred_element_type=F32).astype(BF16)
-            copies[2].start()
-
-    @pl.loop(0, down_blocks)
-    def _(i):
-        block(i, 3)
-
-    for i in range(down_blocks, blocks):
-        block(jnp.int32(i), 2)
-    for i in (blocks - 2, blocks - 1):
-        for copy in writes(jnp.int32(i))[:2]:
-            copy.wait()
-    for i in (down_blocks - 2, down_blocks - 1):
-        writes(jnp.int32(i))[2].wait()
+        down[...] = jnp.dot(act[2, :, at].T, cs[...], preferred_element_type=F32).astype(BF16)
 
 
 def fused(inputs, w_gate, w_up, w_down, cotangent):
@@ -346,17 +313,19 @@
     tokens = 8 * shard
     half, mine, tiles = tokens // 2, tokens // 4, columns // TILE
     dma = pltpu.SemaphoreType.DMA
-    hbm = pl.BlockSpec(memory_space=pl.ANY)
-    xs, cs, act, grad_inputs = pl.pallas_call(
+    hbm, vmem = pl.BlockSpec(memory_space=pl.ANY), pl.BlockSpec(memory_space=pltpu.VMEM)
+    xs, cs, act, own, two, three = pl.pallas_call(
         block_kernel,
         out_shape=(
             jax.ShapeDtypeStruct((tokens, width), BF16),
             jax.ShapeDtypeStruct((tokens, width), BF16),
             jax.ShapeDtypeStruct((3, tokens, columns), BF16),
+            jax.ShapeDtypeStruct((shard, width), F32),
+            jax.ShapeDtypeStruct((shard, width), BF16),
             jax.ShapeDtypeStruct((shard, width), BF16),
         ),
         in_specs=[hbm] * 5,
-        out_specs=(hbm, hbm, hbm, pl.BlockSpec(memory_space=pltpu.VMEM)),
+        out_specs=(hbm, hbm, hbm, vmem, vmem, vmem),
         scratch_shapes=[
             pltpu.VMEM((8, 2, shard, width), BF16),
             pltpu.VMEM(w_gate.shape, BF16),
@@ -373,37 +342,52 @@
             pltpu.VMEM((4, shard, width), F32),
             pltpu.VMEM((4, shard, width), BF16),
             pltpu.VMEM((4, shard, width), BF16),
-            pltpu.VMEM((4, shard, width), BF16),
-            pltpu.VMEM((4, shard, width), BF16),
+            pltpu.VMEM((shard, width), BF16),
+            pltpu.VMEM((shard, width), BF16),
             dma((5,)), dma((3,)), dma((5,)), dma((4,)), dma((4,)), dma((4,)),
             dma((2, tiles)), dma((2, tiles)), dma((2, tiles)), dma((2, tiles)),
             dma((2, tiles)), dma((2, tiles)),
-            dma((4,)), dma((4,)), dma((4,)), dma((4,)),
+            dma((4,)), dma((4,)), dma(()), dma(()),
         ],
         compiler_params=pltpu.CompilerParams(
             collective_id=0, has_side_effects=True, vmem_limit_bytes=56 * 2**20
         ),
         name="swiglu_block",
     )(inputs, cotangent, w_gate, w_up, w_down)
-    vmem = pl.BlockSpec(memory_space=pltpu.VMEM)
+    over_z = [
+        [(2 * z + x, 2 * other + x) for z, other in enumerate(others) for x in range(2)]
+        for others in ((2, 3, 0, 1), (3, 2, 1, 0))
+    ]
+    two = lax.ppermute(two, "col", over_z[0])
+    three = lax.ppermute(three, "col", over_z[1])
+    blocks, down_blocks = width // TILE, columns // TILE
     grad_gate, grad_up, grad_down = pl.pallas_call(
-        weights_kernel,
+        functools.partial(weights_kernel, down_blocks=down_blocks),
+        grid=(blocks,),
         out_shape=(
             jax.ShapeDtypeStruct((width, columns), BF16),
             jax.ShapeDtypeStruct((width, columns), BF16),
             jax.ShapeDtypeStruct((columns, width), BF16),
         ),
-        in_specs=[vmem] * 3,
-        out_specs=(hbm,) * 3,
-        scratch_shapes=[
-            pltpu.VMEM((2, TILE, columns), BF16),
-            pltpu.VMEM((2, TILE, columns), BF16),
-            pltpu.VMEM((2, TILE, width), BF16),
-            dma((3, 2)),
+        in_specs=[
+            pl.BlockSpec((tokens, TILE), lambda i: (0, i)),
+            pl.BlockSpec((tokens, width), lambda i: (0, 0)),
+            pl.BlockSpec((3, tokens, columns), lambda i: (0, 0, 0)),
         ],
-        compiler_params=pltpu.CompilerParams(vmem_limit_bytes=40 * 2**20),
+        out_specs=(
+            pl.BlockSpec((TILE, columns), lambda i: (i, 0)),
+            pl.BlockSpec((TILE, columns), lambda i: (i, 0)),
+            pl.BlockSpec((TILE, width), lambda i: (jnp.minimum(i, down_blocks - 1), 0)),
+        ),
+        compiler_params=pltpu.CompilerParams(vmem_limit_bytes=60 * 2**20),
+        cost_estimate=pl.CostEstimate(
+            flops=6 * tokens * width * columns,
+            bytes_accessed=2 * (3 * width * columns + tokens * (2 * width + 3 * columns)),
+            transcendentals=0,
+        ),
         name="weight_grads",
     )(xs, cs, act)
+    grad_inputs = (own + two.astype(F32) + three.astype(F32)).astype(BF16)
     return grad_inputs, grad_gate, grad_up, grad_down
 
 

time: 83.9 us -> 78.7 us (0.938)
  local copies, waits for them, and re-layouts: 5.38 us -> 0.01 us
  Pallas kernels: 77.6 us -> 74.3 us
  starting transfers between devices: 0 us -> 2.83 us
    pallas_call x1, Pallas kernels: 68.9 us -> 61.2 us  [fused(): pl.pallas_call(block_kernel, out_shape=(jax.ShapeDtypeStruct((tokens, wid...]
    unnamed x7 -> x2, local copies, waits for them, and re-layouts: 5.38 us -> 0.01 us
    pallas_call x1, Pallas kernels: 8.66 us -> 13.2 us  [fused(): pl.pallas_call(functools.partial(weights_kernel, down_blocks=down_blocks)...]
    ppermute x0 -> x2, starting transfers between devices: none -> 2.83 us  [the longest x1 2.32 us: fused(): three = lax.ppermute(three, 'col', over_z[1])]
  transfers between devices with their start and end apart: 0 -> 2, of which waited for: 0 -> 0; matrix products, arithmetic and copies ran while one was open for 0% -> 0% of each run, Pallas kernels for 0% -> 17%
where the time goes in v3:
time: 78.7 us; the launch traced here: 78.5 us
  Pallas kernels  74.3 us (94%)
  starting transfers between devices  2.83 us (4%)
    pallas_call x1, Pallas kernels, fused(): pl.pallas_call(block_kernel, out_shape=(jax.ShapeDtypeStruct((tokens, wid...  61.2 us
    pallas_call x1, Pallas kernels, fused(): pl.pallas_call(functools.partial(weights_kernel, down_blocks=down_blocks)...  13.2 us
    ppermute x1, starting transfers between devices, fused(): three = lax.ppermute(three, 'col', over_z[1])  2.32 us
  transfers between devices with their start and end apart: 2, of which 0 were waited for; matrix products, arithmetic and copies ran while one was open for 0% of the time, Pallas kernels for 17%

profile of v3, /device:TPU:0, one launch (start us, length us, event | category | flops | bytes accessed | tf_op | source)
XLA Modules:
  0.0 78.5 jit_solution(7789906044697966936)
XLA Ops:
  0.6 61.2 %swiglu_block.1 = (bf16[192,2048]{1,0:T(8,128)(2,1)}, bf16[192,2048]{1,0:T(8,128)(2,1)}, bf16[3,192,1792]{2,1,0:T(8,128)(2,1)}, f32[24,2048]{1,0:T(8,128)}, bf16...) custom-call(bf16[24,2048]{1,0:T(8,128)(2,1)} %in_ref.1, bf16[24,2048]{1,0:T(8,128)(2,1)} %cot_ref.1, ...), custom_call_target="tpu_custom_call" | custom-call | tf_op jit(solution)/shard_map/swiglu_block/pallas_call | solution.py:317
  61.8 0.5 collective-permute-start
  62.3 2.3 %collective-permute-start.1 = (bf16[24,2048]{1,0:T(8,128)(2,1)}, bf16[24,2048]{1,0:T(8,128)(2,1)S(1)}, u32[]{:S(2)}, u32[]{:S(2)}) collective-permute-start(bf16[24,2048]{1,0:T(8,128)(2,1)} %get-tuple-element.15), channel_id=1, source_target_pairs={{0,6},{1,7},{2,4},{3,5},{4,2},{5,3},{6,0},{7,1},{8,14},{9,15},{10,... | collective-permute-start | bytes 294920 | tf_op jit(solution)/shard_map/ppermute | solution.py:362
  64.6 0.0 copy-start
  64.6 13.2 %weight_grads.1 = (bf16[2048,1792]{1,0:T(8,128)(2,1)}, bf16[2048,1792]{1,0:T(8,128)(2,1)}, bf16[1792,2048]{1,0:T(8,128)(2,1)}) custom-call(bf16[192,2048]{1,0:T(8,128)(2,1)} %get-tuple-element.16.xs, bf16[192,2048]{1,0:T(8,128)(2,1)} %get-tuple-element.17.cs, bf16[3,192,1792]{2,1,0:T(8,128)(2,1)} %get-tuple-element.18.act), custom_call_target="tpu_custom_call" | custom-call | flops 4227858432 | bytes 25657344 | tf_op jit(solution)/shard_map/weight_grads/pallas_call | solution.py:364
  77.8 0.0 collective-permute-done
  77.8 0.0 collective-permute-done.1
  77.8 0.0 copy-done
  77.8 0.7 add_convert_fusion
Async XLA Ops:
  61.8 16.0 %collective-permute-start = (bf16[24,2048]{1,0:T(8,128)(2,1)}, bf16[24,2048]{1,0:T(8,128)(2,1)S(1)}, u32[]{:S(2)}, u32[]{:S(2)}) collective-permute-start(bf16[24,2048]{1,0:T(8,128)(2,1)} %get-tuple-element.14), channel_id=1, source_target_pairs={{0,4},{1,5},{2,6},{3,7},{4,0},{5,1},{6,2},{7,3},{8,12},{9,13},{10,... | collective-permute-start | bytes 294920 | tf_op jit(solution)/shard_map/ppermute | solution.py:361
  62.3 15.5 %collective-permute-start.1 = (bf16[24,2048]{1,0:T(8,128)(2,1)}, bf16[24,2048]{1,0:T(8,128)(2,1)S(1)}, u32[]{:S(2)}, u32[]{:S(2)}) collective-permute-start(bf16[24,2048]{1,0:T(8,128)(2,1)} %get-tuple-element.15), channel_id=1, source_target_pairs={{0,6},{1,7},{2,4},{3,5},{4,2},{5,3},{6,0},{7,1},{8,14},{9,15},{10,... | collective-permute-start | bytes 294920 | tf_op jit(solution)/shard_map/ppermute | solution.py:362
  64.6 13.2 %copy-start = (f32[24,2048]{1,0:T(8,128)S(1)}, f32[24,2048]{1,0:T(8,128)}, u32[]{:S(2)}) copy-start(f32[24,2048]{1,0:T(8,128)} %get-tuple-element.13) | copy-start | bytes 589828
